TPU v7x, 256 devices: a whole 4x4x8 slice. The times are simulated.
256 devices in a mesh: dp: 16 (over x, y_lo, core), section: 8 (over z), mp: 2 (over y_hi).
Axes of the slice: x: 4, y: 4 (y_hi: 2, y_lo: 2; y = y_hi * 2 + y_lo), z: 8, core: 2. Of those that a mesh axis runs over, the one named last changes fastest.
Arguments:
- enc_states: bfloat16 [8192, 4096], P('dp', ('section', 'mp')), may hold values from -0.0625 to 0.0625
- value_weight: bfloat16 [8, 4096, 2048], P('section', None, 'mp'), may hold values from -0.09375 to 0.09375
- attn_weights: bfloat16 [8, 8, 4096, 512], P('section', 'mp', 'dp'), may hold values from 0 to 1
- ctx_grad: bfloat16 [8, 4096, 2048], P('section', 'dp', 'mp'), may hold values from -0.1796875 to 0.1796875
- prompt_lengths: int32 [16], P('dp'), may hold values from 128 to 512, as said below
Outputs:
- enc_grad: bfloat16 [8192, 4096], P('dp', ('section', 'mp'))
- value_grad: float32 [8, 4096, 2048], P('section', 'dp', 'mp')
Inputs may be any that keep to these rules, and one draw needn't show every extreme that they name: `prompt_lengths`: at least one sequence has the full length 512.
All inputs are finite; a program needn't handle non-finite values.
Results may differ from a plain program's by a relative error of at most 0.005.
Values may be sent and summed in bfloat16 or wider, within the bound.
A program may use at most 128 MiB of HBM per device.

v0:
```python
import jax
import jax.numpy as jnp
from jax import lax
from jax.sharding import PartitionSpec as P


def local(enc_states, value_weight, attn_weights, ctx_grad, prompt_lengths):
    encoded = lax.all_gather(enc_states, ("section", "mp"), axis=1, tiled=True)
    weight = value_weight[0]
    col_count = weight.shape[1]
    head_count = attn_weights.shape[1]
    queries = ctx_grad.shape[1]
    prompt = attn_weights.shape[3]
    grads_ctx = ctx_grad[0].reshape(queries, head_count, col_count // head_count)
    values_raw = jnp.einsum(
        "hqe,qhd->ehd", attn_weights[0], grads_ctx, preferred_element_type=jnp.float32
    )
    keeping = (jnp.arange(prompt, dtype=jnp.int32) < prompt_lengths[0]).astype(jnp.float32)
    value_grads = (values_raw.reshape(prompt, col_count) * keeping[:, None]).astype(jnp.bfloat16)
    partial_enc = lax.dot_general(
        value_grads, weight, (((1,), (1,)), ((), ())), preferred_element_type=jnp.float32
    )
    summed = lax.psum_scatter(partial_enc, ("section", "mp"), scatter_dimension=1, tiled=True)
    enc_grad = summed.astype(jnp.bfloat16)
    weight_grad = lax.psum_scatter(
        lax.dot_general(
            encoded, value_grads, (((0,), (0,)), ((), ())), preferred_element_type=jnp.float32
        ),
        "dp",
        scatter_dimension=0,
        tiled=True,
    )
    return (enc_grad, weight_grad[None])


def solution(mesh):
    in_specs = (
        P("dp", ("section", "mp")),
        P("section", None, "mp"),
        P("section", "mp", "dp", None),
        P("section", "dp", "mp"),
        P("dp"),
    )
    out_specs = (P("dp", ("section", "mp")), P("section", "dp", "mp"))
    return jax.shard_map(local, mesh=mesh, in_specs=in_specs, out_specs=out_specs, check_vma=False)
```

profile of v0, /device:TPU:1, one launch (start us, length us, event | category | flops | bytes accessed | tf_op | source)
XLA Modules:
  0.0 540.3 jit_solution(3993805676401514649)
XLA Ops:
  7.2 0.0 copy-start
  7.2 0.0 all-gather.2.cloned.1.call-start
  7.2 0.7 all-gather.2.cloned.1.call-update
  7.9 0.0 reduce-scatter.3.cloned.1.call-start
  8.6 2.0 copy.9
  10.7 0.0 copy-done
  10.7 1.5 fusion.3
  12.1 10.3 %fusion = f32[512,4096]{1,0:T(8,128)} fusion(bf16[512,1024]{0,1:T(8,128)(2,1)S(1)} %bitcast.30, bf16[1,4096,1024]{2,1,0:T(8,128)(2,1)} %param.6), kind=kOutput, calls=%fused_computation.1 | convolution fusion | flops 4294967296 | bytes 17825792 | tf_op jit(solution)/shard_map/dot_general | solution.py:20
  22.4 0.0 reduce-scatter.3.cloned.1.call-update
  22.5 0.0 reduce-scatter.5.cloned.1.call-start
  22.5 1.3 fusion.2
  23.8 92.5 %all-gather.2.cloned.1.call-done = bf16[512,4096]{1,0:T(8,128)(2,1)} async-done(((bf16[512,256]{1,0:T(8,128)(2,1)}), bf16[512,4096]{1,0:T(8,128)(2,1)}) %all-gather.2.cloned.1.call-update) | async-done | bytes 4194320 | tf_op jit(solution)/shard_map/all_gather | solution.py:8
  116.2 12.7 %convolution_bitcast_fusion = f32[4096,1024]{0,1:T(8,128)} fusion(bf16[512,1024]{0,1:T(8,128)(2,1)} %fusion.2, bf16[512,4096]{1,0:T(8,128)(2,1)} %all-gather.2.cloned.1.call-done), kind=kOutput, calls=%fused_computation | convolution fusion | flops 4294967296 | bytes 22020096 | tf_op jit(solution)/shard_map/dot_general | solution.py:26
  129.0 0.0 reduce-scatter.5.cloned.1.call-update
  129.0 213.8 %reduce-scatter.3.cloned.1.call-done = f32[512,256]{1,0:T(8,128)} async-done(((f32[512,4096]{1,0:T(8,128)}), f32[512,256]{1,0:T(8,128)}) %reduce-scatter.3.cloned.1.call-update) | async-done | bytes 524304 | tf_op jit(solution)/shard_map/reduce_scatter | solution.py:23
  342.8 1.8 convert_element_type.21
  344.6 186.7 %reduce-scatter.5.cloned.1.call-done = f32[256,1024]{0,1:T(8,128)} async-done(((f32[4096,1024]{0,1:T(8,128)}), f32[256,1024]{0,1:T(8,128)}) %reduce-scatter.5.cloned.1.call-update) | async-done | bytes 1048592 | tf_op jit(solution)/shard_map/reduce_scatter | solution.py:25
  531.3 2.5 copy.8
  (1 shorter events, 0.0 us)
Async XLA Ops:
  7.2 3.5 copy-start
  7.2 109.1 %all-gather.2.cloned.1.call-start = ((), (), s32[]{:S(2)}) async-start(), calls=%async_computation.3 | async-start | bytes 4456448 | tf_op jit(solution)/shard_map/all_gather | solution.py:8
  7.9 334.9 %reduce-scatter.3.cloned.1.call-start = ((), (), s32[]{:S(2)}) async-start(), calls=%async_computation.2 | async-start | bytes 8912896 | tf_op jit(solution)/shard_map/reduce_scatter | solution.py:23
  22.5 508.8 %reduce-scatter.5.cloned.1.call-start = ((), (), s32[]{:S(2)}) async-start(), calls=%async_computation.4 | async-start | bytes 17825792 | tf_op jit(solution)/shard_map/reduce_scatter | solution.py:25
Sparse Core Ops, SparseCore 0:
  10.5 105.6 all-gather.1
  120.3 222.4 reduce-scatter.2
  345.4 185.8 reduce-scatter.4
where the time goes:
time: 541 us; the launch traced here: 540 us
  waiting for transfers between devices  494 us (91%)
  matrix products  24.5 us (5%)
  between operations  14.4 us (3%)
    reduce_scatter x1, waiting for transfers between devices, local(): lax.psum_scatter(partial_enc, ('section', 'mp'), scatter_dimension=1, til...  214 us
    reduce_scatter x1, waiting for transfers between devices, local(): lax.psum_scatter(lax.dot_general(encoded, value_grads, (((0,), (0,)), (()...  187 us
    all_gather x1, waiting for transfers between devices, local(): encoded = lax.all_gather(enc_states, ('section', 'mp'), axis=1, tiled=True)  92.5 us
    dot_general x1, matrix products, local(): lax.dot_general(encoded, value_grads, (((0,), (0,)), ((), ())), preferred...  12.7 us
  transfers between devices with their start and end apart: 3, of which 3 were waited for; matrix products, arithmetic and copies ran while one was open for 5% of the time, Pallas kernels for 0%

commit v1 on v0

v1 whole, which is shorter than its diff:
```python
import jax
import jax.numpy as jnp
from jax import lax
from jax.experimental import pallas as pl
from jax.experimental.pallas import tpu as pltpu
from jax.sharding import PartitionSpec as P


MESH = pl.DeviceIdType.MESH
REL = (4, 3, 5, 2, 6, 1, 7, 0)
POS = {rel: slot for slot, rel in enumerate(REL)}
BF16 = jnp.bfloat16
F32 = jnp.float32


def dot(a, b, ca, cb):
    return lax.dot_general(a, b, (((ca,), (cb,)), ((), ())), preferred_element_type=F32)


def kernel(
    lens, enc, weight, attn, ctx, eg_out, vg_out,
    attn_v, ctx_v, ebuf, et, val, wq, zsum, zs, zr, gkeep, gs, gr, xs, xr, fs, fr,
    lsem, wlsem, essem, ersem, vssem, vrsem, wssem, wrsem, zssem, zrsem,
    gssem, grsem, xssem, xrsem, fssem, frsem, ossem, orsem,
):
    dp, z, m = lax.axis_index("dp"), lax.axis_index("section"), lax.axis_index("mp")
    x, s, c = dp // 4, (dp // 2) % 2, dp % 2

    def dev(x_, s_, c_, z_, m_):
        return (x_ * 4 + s_ * 2 + c_, z_, m_)

    n1 = dev(x, 1 - s, c, z, m)
    n2 = dev(x, 1 - s, c, z, 1 - m)
    peer = dev(x, s, 1 - c, z, m)
    zdev = (dev(x, s, c, (z + 1) % 8, m), dev(x, s, c, (z + 7) % 8, m))
    xdev = tuple(dev((x + k) % 4, s, c, z, m) for k in (1, 2, 3))
    selfy = jnp.logical_and(s == c, c == m)
    same = selfy.astype(jnp.int32)
    sends = []

    def remote(src, dst, ss, rs, where):
        return pltpu.make_async_remote_copy(
            src_ref=src, dst_ref=dst, send_sem=ss, recv_sem=rs, device_id=where, device_id_type=MESH
        )

    def go(copy):
        copy.start()
        sends.append(copy)

    own_enc = pltpu.make_async_copy(
        enc.at[:, pl.ds(pl.multiple_of(s * 128, 128), 128)], ebuf.at[0, 0], lsem.at[0]
    )
    own_attn = pltpu.make_async_copy(attn.at[0], attn_v, lsem.at[1])
    own_ctx = pltpu.make_async_copy(ctx.at[0], ctx_v, lsem.at[2])
    own_enc.start()
    own_ctx.start()
    own_attn.start()

    def weight_rows(slot_rel, m_, s_):
        layer = (z + slot_rel) % 8
        return pl.ds(pl.multiple_of((2 * layer + m_) * 256 + s_ * 128, 128), 128)

    own_w = []
    for slot in range(8):
        own_w.append(
            pltpu.make_async_copy(
                weight.at[0, weight_rows(REL[slot], m, s), :], wq.at[0, pl.ds(slot * 128, 128), :], wlsem.at[slot]
            )
        )

    barrier = pltpu.get_barrier_semaphore()
    for where in (n1, n2, peer) + zdev + xdev:
        pl.semaphore_signal(barrier, inc=1, device_id=where, device_id_type=MESH)
    for half in range(2):
        @pl.when(jnp.logical_not(jnp.logical_and(selfy, s == half)))
        def _():
            pl.semaphore_signal(barrier, inc=1, device_id=dev(x, half, s, z, c), device_id_type=MESH)
    pl.semaphore_wait(barrier, 10 - same)

    pre = remote(
        enc.at[:, pl.ds(pl.multiple_of((1 - s) * 128, 128), 128)], ebuf.at[1, 0], essem.at[1, 0], ersem.at[1, 0], n1
    )
    go(pre)
    own_enc.wait()

    ecopy = {}
    for part in range(2):
        for direction in range(2):
            for step in range(4 if part == direction else 3):
                src = (8 - step) % 8 if direction else step
                to = 7 - step if direction else step + 1
                ecopy[part, to] = remote(
                    ebuf.at[part, src], ebuf.at[part, to], essem.at[part, to], ersem.at[part, to], zdev[direction]
                )
    go(ecopy[0, 1])
    go(ecopy[0, 7])

    piece = 2 * x + c
    piece_rel = 0
    for slot in range(8):
        piece_rel = jnp.where(piece == slot, REL[slot], piece_rel)
    piece_rows = pl.ds(pl.multiple_of(piece * 128, 128), 128)
    w_in = remote(
        weight.at[0, weight_rows(piece_rel, 1 - m, 1 - s), :], wq.at[1, piece_rows, :], wssem.at[0], wrsem.at[0], n2
    )
    go(w_in)
    for copy in own_w:
        copy.start()

    own_ctx.wait()
    own_attn.wait()
    keep = (lax.broadcasted_iota(jnp.int32, (512, 256), 0) < lens[0]).astype(F32)
    vcopy = {}
    for h in range(4):
        vcopy[1, h] = remote(val.at[0, h], val.at[1, h], vssem.at[1, h], vrsem.at[1, h], n1)
        vcopy[3, h] = remote(val.at[0, h], val.at[3, h], vssem.at[3, h], vrsem.at[3, h], n2)
        if h < 2:
            vcopy[2, h] = remote(val.at[3, h], val.at[2, h], vssem.at[2, h], vrsem.at[2, h], n1)
        else:
            vcopy[2, h] = remote(val.at[1, h], val.at[2, h], vssem.at[2, h], vrsem.at[2, h], n2)
        raw = dot(attn_v[h], ctx_v[:, h * 256 : (h + 1) * 256], 0, 0)
        val[0, h] = (raw * keep).astype(BF16)
        go(vcopy[1, h])
        go(vcopy[3, h])

    def put_et(part, rel):
        layer = (z + 8 - rel) % 8
        row = ((layer + c) % 2 * 4 + (layer // 2 + 4 - x) % 4) * 128
        et[part, pl.ds(pl.multiple_of(row, 128), 128), :] = ebuf[part, rel].T

    def enc_in(part, rel):
        ecopy[part, rel].wait_recv()
        following = rel - 1 if rel > 4 or (rel == 4 and part == 1) else rel + 1
        if (part, following) in ecopy and 0 < following < 8:
            up = rel < 4 or (rel == 4 and part == 0)
            if (up and following <= (4 if part == 0 else 3)) or (not up and following >= (5 if part == 0 else 4)):
                go(ecopy[part, following])
        put_et(part, rel)

    def value_in(h):
        vcopy[3, h].wait_recv()
        if h < 2:
            go(vcopy[2, h])
        vcopy[1, h].wait_recv()
        if h >= 2:
            go(vcopy[2, h])

    def z_part(part, pair, which, first):
        slot = {(0, 0): 0, (0, 1): 2, (1, 0): 1, (1, 1): 3}[part, which]
        rows = wq.at[which, pl.ds(pair * 256, 256), :]
        acc = None
        for h in range(4):
            term = dot(val[slot, h], rows[:, h * 256 : (h + 1) * 256], 1, 1)
            acc = term if acc is None else acc + term
        for i in range(2):
            half = acc[:, i * 128 : (i + 1) * 128]
            if first:
                zsum[part, 2 * pair + i] = half
            else:
                zsum[part, 2 * pair + i] += half

    put_et(0, 0)
    pre.wait_recv()
    go(ecopy[1, 1])
    go(ecopy[1, 7])
    put_et(1, 0)
    enc_in(0, 1)
    enc_in(0, 7)
    for copy in own_w:
        copy.wait()
    for pair in range(4):
        z_part(0, pair, 0, True)
    enc_in(1, 1)
    enc_in(1, 7)

    w_in.wait_recv()
    piece_ref = wq.at[1, piece_rows, :]
    w_x = [remote(piece_ref, piece_ref, wssem.at[1 + k], wrsem.at[1 + k], xdev[k]) for k in range(3)]
    w_c = []
    for k in range(4):
        there = (x + 4 - k) % 4
        ref = wq.at[1, pl.ds(pl.multiple_of((2 * there + c) * 128, 128), 128), :]
        w_c.append(remote(ref, ref, wssem.at[4 + k], wrsem.at[4 + k], peer))
    for copy in w_x:
        go(copy)
    go(w_c[0])
    value_in(0)
    enc_in(0, 2)
    enc_in(0, 6)
    enc_in(1, 2)
    enc_in(1, 6)
    value_in(1)
    enc_in(0, 3)
    enc_in(0, 5)
    value_in(2)
    enc_in(1, 3)
    enc_in(1, 5)
    for k in (0, 2, 1):
        w_x[k].wait_recv()
        go(w_c[k + 1])
    enc_in(0, 4)
    enc_in(1, 4)
    for k in range(4):
        w_c[k].wait_recv()
    value_in(3)

    STREAMS = ((0, 0), (0, 1), (1, 1), (1, 0))
    zcopy = {}
    for part in range(2):
        for direction, half in STREAMS:
            for step in range(4 if direction == half else 3):
                zcopy[part, direction, half, step] = remote(
                    zs.at[part, direction, half, step], zr.at[part, direction, half, step],
                    zssem.at[part, direction, half, step], zrsem.at[part, direction, half, step], zdev[direction],
                )

    def z_step(part, direction, half, step):
        length = 4 if direction == half else 3
        if step >= length:
            return
        ahead = length - step
        slot = POS[(8 - ahead) % 8 if direction else ahead]
        value = zsum[part, slot, half * 256 : (half + 1) * 256, :]
        if step > 0:
            zcopy[part, direction, half, step - 1].wait_recv()
            value = value + zr[part, direction, half, step - 1].astype(F32)
        zs[part, direction, half, step] = value.astype(BF16)
        go(zcopy[part, direction, half, step])

    def z_all(part, step):
        for direction, half in STREAMS:
            z_step(part, direction, half, step)

    col_mine = pl.ds(pl.multiple_of(s * 128, 128), 128)

    gcopy = [remote(gs.at[i], gr.at[i], gssem.at[i], grsem.at[i], peer) for i in range(8)]

    def g_head(f, h):
        i = f * 4 + h
        va, vb = (0, 1) if f == 0 else (2, 3)
        gs[i] = (dot(et[0, 512:, :], val[va, h], 1, 0) + dot(et[1, 512:, :], val[vb, h], 1, 0)).astype(BF16)
        go(gcopy[i])
        gkeep[i] = dot(et[0, :512, :], val[va, h], 1, 0) + dot(et[1, :512, :], val[vb, h], 1, 0)

    xcopy = {}
    for q in range(4):
        for k in range(3):
            xcopy[q, k] = remote(xs.at[q, k], xr.at[q, k], xssem.at[q, k], xrsem.at[q, k], xdev[k])

    def x_send(f, p):
        q = f * 2 + p
        for j in range(2):
            gcopy[f * 4 + p + 2 * j].wait_recv()
        for k in (1, 0, 2):
            for j in range(2):
                i = f * 4 + p + 2 * j
                rows = slice((k + 1) * 128, (k + 2) * 128)
                xs[q, k, j] = (gkeep[i, rows, :] + gr[i, rows, :].astype(F32)).astype(BF16)
            go(xcopy[q, k])

    fcopy = {}
    for q in range(4):
        fcopy[q] = remote(
            fs.at[q], fr.at[s, q % 2], fssem.at[q], frsem.at[s, q % 2], dev(x, c, m, z, m if q < 2 else 1 - m)
        )

    def f_send(f, p):
        q = f * 2 + p
        for k in range(3):
            xcopy[q, k].wait_recv()
        for j in range(2):
            i = f * 4 + p + 2 * j
            value = gkeep[i, :128, :] + gr[i, :128, :].astype(F32)
            for k in range(3):
                value = value + xr[q, k, j].astype(F32)
            fs[q, j] = value.astype(BF16)
        if f == 0:
            @pl.when(selfy)
            def _():
                fr[s, p] = fs[q]

            @pl.when(jnp.logical_not(selfy))
            def _():
                fcopy[q].start()
        else:
            go(fcopy[q])

    for pair in range(4):
        z_part(1, pair, 0, True)
        z_part(1, pair, 1, False)
        if pair == 0:
            z_step(1, 0, 0, 0)
            z_step(1, 1, 1, 0)
            z_step(1, 0, 1, 0)
        if pair == 1:
            z_step(1, 1, 0, 0)
    g_head(0, 0)
    g_head(0, 2)
    z_all(1, 1)
    x_send(0, 0)
    g_head(0, 1)
    g_head(0, 3)
    z_all(1, 2)
    x_send(0, 1)
    z_all(1, 3)
    vcopy[2, 0].wait_recv()
    g_head(1, 0)
    vcopy[2, 2].wait_recv()
    g_head(1, 2)
    x_send(1, 0)
    f_send(0, 0)
    vcopy[2, 1].wait_recv()
    vcopy[2, 3].wait_recv()
    for pair in range(4):
        z_part(0, pair, 1, False)
        if pair == 0:
            z_step(0, 0, 0, 0)
            z_step(0, 1, 1, 0)
            z_step(0, 0, 1, 0)
        if pair == 1:
            z_step(0, 1, 0, 0)
    g_head(1, 1)
    g_head(1, 3)
    z_all(0, 1)
    x_send(1, 1)
    for half in range(2):
        rows = slice(half * 256, (half + 1) * 256)
        value = zsum[1, POS[0], rows, :]
        for direction in range(2):
            step = (4 if direction == half else 3) - 1
            zcopy[1, direction, half, step].wait_recv()
            value = value + zr[1, direction, half, step].astype(F32)
        et[0, half * 256 : (half + 1) * 256, :128] = value.astype(BF16)
    out_copy = remote(et.at[0, pl.ds(0, 512), pl.ds(0, 128)], eg_out.at[:, col_mine], ossem.at[0], orsem.at[0], n1)
    go(out_copy)
    z_all(0, 2)
    f_send(0, 1)
    z_all(0, 3)
    f_send(1, 0)
    for half in range(2):
        rows = slice(half * 256, (half + 1) * 256)
        value = zsum[0, POS[0], rows, :]
        for direction in range(2):
            step = (4 if direction == half else 3) - 1
            zcopy[0, direction, half, step].wait_recv()
            value = value + zr[0, direction, half, step].astype(F32)
        eg_out[rows, col_mine] = value.astype(BF16)
    f_send(1, 1)

    for p in range(2):
        for half in range(2):
            @pl.when(jnp.logical_not(jnp.logical_and(selfy, s == half)))
            def _():
                remote(fs.at[p], fr.at[half, p], fssem.at[p], frsem.at[half, p], n1).wait_recv()
            for j in range(2):
                h = p + 2 * j
                vg_out[0, half * 128 : (half + 1) * 128, h * 256 : (h + 1) * 256] = fr[half, p, j].astype(F32)
    out_copy.wait_recv()
    for copy in sends:
        copy.wait_send()
    for q in range(2):
        @pl.when(jnp.logical_not(selfy))
        def _():
            fcopy[q].wait_send()


def local(enc_states, value_weight, attn_weights, ctx_grad, prompt_lengths):
    anywhere = pl.BlockSpec(memory_space=pl.ANY)
    vmem = pl.BlockSpec(memory_space=pltpu.VMEM)
    dma = pltpu.SemaphoreType.DMA
    enc_grad, value_grad = pl.pallas_call(
        kernel,
        out_shape=(jax.ShapeDtypeStruct((512, 256), BF16), jax.ShapeDtypeStruct((1, 256, 1024), F32)),
        in_specs=[pl.BlockSpec(memory_space=pltpu.SMEM)] + [anywhere] * 4,
        out_specs=(vmem, vmem),
        scratch_shapes=[
            pltpu.VMEM((4, 256, 512), BF16),
            pltpu.VMEM((256, 1024), BF16),
            pltpu.VMEM((2, 8, 512, 128), BF16),
            pltpu.VMEM((2, 1024, 512), BF16),
            pltpu.VMEM((4, 4, 512, 256), BF16),
            pltpu.VMEM((2, 1024, 1024), BF16),
            pltpu.VMEM((2, 8, 512, 128), F32),
            pltpu.VMEM((2, 2, 2, 4, 256, 128), BF16),
            pltpu.VMEM((2, 2, 2, 4, 256, 128), BF16),
            pltpu.VMEM((8, 512, 256), F32),
            pltpu.VMEM((8, 512, 256), BF16),
            pltpu.VMEM((8, 512, 256), BF16),
            pltpu.VMEM((4, 3, 2, 128, 256), BF16),
            pltpu.VMEM((4, 3, 2, 128, 256), BF16),
            pltpu.VMEM((4, 2, 128, 256), BF16),
            pltpu.VMEM((2, 2, 2, 128, 256), BF16),
            dma((3,)), dma((8,)),
            dma((2, 8)), dma((2, 8)),
            dma((4, 4)), dma((4, 4)),
            dma((8,)), dma((8,)),
            dma((2, 2, 2, 4)), dma((2, 2, 2, 4)),
            dma((8,)), dma((8,)),
            dma((4, 3)), dma((4, 3)),
            dma((4,)), dma((2, 2)),
            dma((1,)), dma((1,)),
        ],
        compiler_params=pltpu.CompilerParams(
            collective_id=0, has_side_effects=True, vmem_limit_bytes=60 * 2**20
        ),
        cost_estimate=pl.CostEstimate(flops=9 * 10**9, bytes_accessed=12 * 2**20, transcendentals=0),
    )(prompt_lengths, enc_states, value_weight, attn_weights, ctx_grad)
    return enc_grad, value_grad


def solution(mesh):
    in_specs = (
        P("dp", ("section", "mp")),
        P("section", None, "mp"),
        P("section", "mp", "dp", None),
        P("section", "dp", "mp"),
        P("dp"),
    )
    out_specs = (P("dp", ("section", "mp")), P("section", "dp", "mp"))
    return jax.shard_map(local, mesh=mesh, in_specs=in_specs, out_specs=out_specs, check_vma=False)
```

time: 541 us -> 88.7 us (0.16)
  waiting for transfers between devices: 494 us -> 0 us
  Pallas kernels: 0 us -> 83.2 us
  matrix products: 24.5 us -> 0 us
  between operations: 14.4 us -> 1.29 us
    reduce_scatter x2 -> x0, waiting for transfers between devices: 400 us -> none  [the longest x1 214 us: local(): lax.psum_scatter(partial_enc, ('section', 'mp'), scatter_dimension=1, til...]
    all_gather x1 -> x0, waiting for transfers between devices: 92.5 us -> none  [local(): encoded = lax.all_gather(enc_states, ('section', 'mp'), axis=1, tiled=True)]
    pallas_call x0 -> x1, Pallas kernels: none -> 83.2 us  [local(): pl.pallas_call(kernel, out_shape=(jax.ShapeDtypeStruct((512, 256), BF16),...]
    dot_general x3 -> x0, matrix products: 24.5 us -> none  [the longest x1 12.7 us: local(): lax.dot_general(encoded, value_grads, (((0,), (0,)), ((), ())), preferred...]
  transfers between devices with their start and end apart: 3 -> 0, of which waited for: 3 -> 0; matrix products, arithmetic and copies ran while one was open for 5% -> 0% of each run, Pallas kernels for 0% -> 0%
where the time goes in v1:
time: 88.7 us; the launch traced here: 88.5 us
  Pallas kernels  83.2 us (94%)
  local copies, waits for them, and re-layouts  3.98 us (4%)
  between operations  1.29 us (1%)
    pallas_call x1, Pallas kernels, local(): pl.pallas_call(kernel, out_shape=(jax.ShapeDtypeStruct((512, 256), BF16),...  83.2 us
    unnamed x2, local copies, waits for them, and re-layouts  3.98 us

profile of v1, /device:TPU:1, one launch (start us, length us, event | category | flops | bytes accessed | tf_op | source)
XLA Modules:
  0.0 88.5 jit_solution(15937312050798634088)
XLA Ops:
  1.3 83.2 %shard_map.68 = (bf16[512,256]{1,0:T(8,128)(2,1)}, f32[1,256,1024]{2,1,0:T(8,128)}) custom-call(s32[1]{0:T(128)S(6)} %copy.9.lens, bf16[512,256]{1,0:T(8,128)(2,1)} %enc.1, bf16[1,4096,1024]{2,1,0:T(8,128)(2,1)} %weight.1, bf16[1,4,256,512]{3,2,1,0:T(8,128)(2,1)} %attn.1, bf16[1,256,1024]{2,1,0:T(8,128)(2,1)} %ctx.1), custom_call_target="tpu_custom_call" | custom-call | flops 8999999488 | bytes 12582912 | tf_op jit(solution)/shard_map/pallas_call | solution.py:371
  84.5 1.7 %copy.10 = bf16[512,256]{1,0:T(8,128)(2,1)} copy(bf16[512,256]{1,0:T(8,128)(2,1)} %get-tuple-element.4) | data formatting | bytes 524288
  86.2 2.3 %copy.11 = f32[1,256,1024]{2,1,0:T(8,128)} copy(f32[1,256,1024]{2,1,0:T(8,128)} %get-tuple-element.5) | data formatting | bytes 2097152

commit v2 on v0

v2 whole, which is shorter than its diff:
```python
import jax
import jax.numpy as jnp
from jax import lax
from jax.experimental import pallas as pl
from jax.experimental.pallas import tpu as pltpu
from jax.sharding import PartitionSpec as P


MESH = pl.DeviceIdType.MESH
REL = (4, 3, 5, 2, 6, 1, 7, 0)
POS = {rel: slot for slot, rel in enumerate(REL)}
BF16 = jnp.bfloat16
F32 = jnp.float32
WINDOW = 3
ORDER = (
    ("v", 3, 1), ("second", 0), ("et", 0, 0), ("zf", 0, 0), ("e", 0, 1, 0), ("e", 0, 7, 0), ("zf", 0, 1), ("won", 0),
    ("v", 3, 2), ("v", 1, 3), ("second", 1), ("et", 1, 0), ("e", 0, 1, 1), ("e", 0, 7, 1), ("e", 1, 7, 0),
    ("e", 1, 1, 0), ("won", 1), ("v", 3, 3), ("v", 1, 4), ("e", 0, 6, 0), ("e", 0, 2, 0), ("e", 1, 1, 1),
    ("e", 1, 7, 1), ("v", 1, 5), ("v", 3, 4), ("wac", 1, 0), ("e", 0, 2, 1), ("e", 0, 6, 1), ("e", 1, 2, 0),
    ("e", 1, 6, 0), ("v", 1, 6), ("v", 3, 5), ("wac", 2, 0), ("wac", 0, 0), ("e", 0, 5, 0), ("e", 0, 3, 0),
    ("e", 1, 2, 1), ("zf", 1, 0), ("wac", 1, 1), ("v", 1, 7), ("v", 3, 6), ("e", 1, 6, 1), ("e", 0, 3, 1),
    ("e", 0, 5, 1), ("e", 1, 5, 0), ("e", 1, 3, 0), ("v", 1, 8), ("v", 3, 7), ("wac", 2, 1), ("wac", 0, 1),
    ("e", 0, 4, 0), ("wdone",), ("zs", 1, 0), ("e", 1, 3, 1), ("e", 1, 5, 1), ("v", 1, 9), ("v", 3, 8),
    ("e", 0, 4, 1), ("e", 1, 4, 0), ("v", 1, 10), ("v", 3, 9), ("z", 1, 1, 0, 1), ("z", 1, 0, 0, 1),
    ("z", 1, 0, 1, 1), ("z", 1, 1, 1, 1), ("e", 1, 4, 1), ("g", 0, 0), ("g", 0, 1), ("z", 1, 0, 0, 2),
    ("z", 1, 0, 1, 2), ("v", 3, 10), ("x", 0, 0), ("zf", 1, 1), ("v", 3, 11), ("x", 0, 1), ("v", 1, 11),
    ("z", 1, 1, 0, 2), ("z", 1, 1, 1, 2), ("g", 0, 3), ("zs", 1, 1), ("z", 1, 0, 0, 3), ("g", 0, 2), ("x", 0, 3),
    ("g", 1, 0), ("x", 0, 2), ("g", 1, 1), ("z", 1, 1, 3, 1), ("z", 1, 1, 2, 1), ("x", 1, 0), ("z", 1, 0, 2, 1),
    ("f", 0, 1), ("z", 1, 0, 3, 1), ("zs", 0, 0), ("z", 1, 1, 1, 3), ("f", 0, 0), ("g", 1, 2), ("z", 1, 1, 3, 2),
    ("zs", 0, 1), ("z", 1, 1, 2, 2), ("z", 1, 0, 3, 2), ("x", 1, 2), ("z", 1, 0, 2, 2), ("z", 0, 1, 0, 1),
    ("f", 0, 3), ("z", 0, 0, 0, 1), ("x", 1, 1), ("z", 0, 0, 1, 1), ("f", 0, 2), ("z", 0, 1, 1, 1), ("ze", 1, 0),
    ("g", 1, 3), ("z", 1, 1, 3, 3), ("z", 0, 1, 2, 1), ("z", 0, 0, 2, 1), ("z", 0, 0, 3, 1), ("z", 0, 1, 3, 1),
    ("f", 1, 0), ("x", 1, 3), ("z", 1, 0, 2, 3), ("z", 0, 1, 0, 2), ("z", 0, 0, 0, 2), ("z", 0, 1, 1, 2),
    ("z", 0, 0, 1, 2), ("f", 1, 2), ("z", 0, 0, 2, 2), ("z", 0, 1, 2, 2), ("fin", 0), ("z", 0, 0, 3, 2),
    ("z", 0, 1, 3, 2), ("ze", 1, 1), ("out",), ("z", 0, 0, 0, 3), ("f", 1, 1), ("z", 0, 1, 1, 3), ("fin", 2),
    ("z", 0, 0, 2, 3), ("z", 0, 1, 3, 3), ("f", 1, 3), ("ze", 0, 0), ("fin", 1), ("ze", 0, 1), ("fin", 3),
)


def dot(a, b, ca, cb):
    return lax.dot_general(a, b, (((ca,), (cb,)), ((), ())), preferred_element_type=F32)


def kernel(
    lens, enc, weight, attn, ctx, enc_out, val_out,
    attn_v, ctx_v, ebuf, et, val, wq, zsum, zs, zr, gkeep, gs, gr, xs, xr, fs, zout,
    lsem, wlsem, essem, ersem, vssem, vrsem, wssem, wrsem, zssem, zrsem,
    gssem, grsem, xssem, xrsem, fssem, frsem, ossem, orsem,
):
    dp, z, m = lax.axis_index("dp"), lax.axis_index("section"), lax.axis_index("mp")
    x, s, c = dp // 4, (dp // 2) % 2, dp % 2

    def dev(x_, s_, c_, z_, m_):
        return (x_ * 4 + s_ * 2 + c_, z_, m_)

    n1 = dev(x, 1 - s, c, z, m)
    n2 = dev(x, 1 - s, c, z, 1 - m)
    peer = dev(x, s, 1 - c, z, m)
    zdev = (dev(x, s, c, (z + 1) % 8, m), dev(x, s, c, (z + 7) % 8, m))
    xdev = tuple(dev((x + k) % 4, s, c, z, m) for k in (1, 2, 3))
    selfy = jnp.logical_and(s == c, c == m)
    same = selfy.astype(jnp.int32)
    sends = []

    def remote(src, dst, ss, rs, where):
        return pltpu.make_async_remote_copy(
            src_ref=src, dst_ref=dst, send_sem=ss, recv_sem=rs, device_id=where, device_id_type=MESH
        )

    def go(copy):
        copy.start()
        sends.append(copy)

    def sent(copy):
        copy.wait_send()
        sends[:] = [other for other in sends if other is not copy]

    own_enc = pltpu.make_async_copy(
        enc.at[:, pl.ds(pl.multiple_of(s * 128, 128), 128)], ebuf.at[0, 0], lsem.at[0]
    )
    own_ctx = pltpu.make_async_copy(ctx.at[0], ctx_v, lsem.at[1])
    own_attn = [pltpu.make_async_copy(attn.at[0, h], attn_v.at[h], lsem.at[2 + h]) for h in range(4)]
    own_enc.start()
    own_attn[0].start()
    own_ctx.start()
    for h in range(1, 4):
        own_attn[h].start()

    def weight_rows(slot_rel, m_, s_):
        layer = (z + slot_rel) % 8
        return pl.ds(pl.multiple_of((2 * layer + m_) * 256 + s_ * 128, 128), 128)

    own_w = []
    for slot in range(8):
        own_w.append(
            pltpu.make_async_copy(
                weight.at[0, weight_rows(REL[slot], m, s), :], wq.at[0, pl.ds(slot * 128, 128), :], wlsem.at[slot]
            )
        )

    barrier = pltpu.get_barrier_semaphore()
    for where in (n1, n2, peer) + zdev + xdev:
        pl.semaphore_signal(barrier, inc=1, device_id=where, device_id_type=MESH)
    for half in range(2):
        @pl.when(jnp.logical_not(jnp.logical_and(selfy, s == half)))
        def _():
            pl.semaphore_signal(barrier, inc=1, device_id=dev(x, half, s, z, c), device_id_type=MESH)
    pl.semaphore_wait(barrier, 10 - same)

    row_half = (pl.ds(0, 256), pl.ds(256, 256))
    pre = []
    for u in range(2):
        src = enc.at[row_half[u], pl.ds(pl.multiple_of((1 - s) * 128, 128), 128)]
        pre.append(remote(src, ebuf.at[1, 0, row_half[u], :], essem.at[1, 0, u], ersem.at[1, 0, u], n1))
        go(pre[u])
    own_enc.wait()

    ecopy = {}
    for part in range(2):
        for u in range(2):
            for direction in range(2):
                for step in range(4 if (part == u) == (direction == 0) else 3):
                    src = (8 - step) % 8 if direction else step
                    to = 7 - step if direction else step + 1
                    ecopy[part, to, u] = remote(
                        ebuf.at[part, src, row_half[u], :], ebuf.at[part, to, row_half[u], :],
                        essem.at[part, to, u], ersem.at[part, to, u], zdev[direction],
                    )
    for u in range(2):
        go(ecopy[0, 1, u])
        go(ecopy[0, 7, u])

    piece = 2 * x + c
    piece_rel = 0
    for slot in range(8):
        piece_rel = jnp.where(piece == slot, REL[slot], piece_rel)
    layer_rows = (2 * ((z + piece_rel) % 8) + 1 - m) * 256 + (1 - s) * 128

    def weight_piece(owner, j):
        return wq.at[1, pl.ds(pl.multiple_of(owner * 128 + j * 64, 64), 64), :]

    w_in = []
    for j in range(2):
        rows = pl.ds(pl.multiple_of(layer_rows + j * 64, 64), 64)
        w_in.append(remote(weight.at[0, rows, :], weight_piece(piece, j), wssem.at[0, j], wrsem.at[0, j], n2))
        go(w_in[j])
    for copy in own_w:
        copy.start()


    def value_copy(src, to, h, t, where):
        return remote(
            val.at[src, h, row_half[t], :], val.at[to, h, row_half[t], :],
            vssem.at[to, h, t], vrsem.at[to, h, t], where,
        )

    vcopy = {}
    for h in range(4):
        for t in range(2):
            vcopy[1, h, t] = value_copy(0, 1, h, t, n1)
            vcopy[3, h, t] = value_copy(0, 3, h, t, n2)
            vcopy[2, h, t] = value_copy(3, 2, h, t, n1) if t == 0 else value_copy(1, 2, h, t, n2)
    queues = {}
    for to, through in ((1, 0), (3, 1)):
        queues[to] = [(to, h, t) for t in range(2) for h in range(4)] + [(2, h, through) for h in range(4)]
    arrived = set()

    def value_in(*key):
        if key not in arrived:
            arrived.add(key)
            vcopy[key].wait_recv()

    def value_next(to, i):
        if i >= WINDOW:
            sent(vcopy[queues[to][i - WINDOW]])
        key = queues[to][i]
        if key[0] == 2:
            value_in(4 - to, key[1], key[2])
        go(vcopy[key])

    own_ctx.wait()
    keep = (lax.broadcasted_iota(jnp.int32, (512, 256), 0) < lens[0]).astype(F32)
    for h in range(4):
        own_attn[h].wait()
        raw = dot(attn_v[h], ctx_v[:, h * 256 : (h + 1) * 256], 0, 0)
        val[0, h] = (raw * keep).astype(BF16)
        if h < WINDOW:
            value_next(1, h)
        if h == 0:
            value_next(3, 0)

    def put_et(part, rel, u):
        layer = (z + 8 - rel) % 8
        row = ((layer + c) % 2 * 4 + (layer // 2 + 4 - x) % 4) * 128
        columns = slice(u * 256, (u + 1) * 256)
        et[part, pl.ds(pl.multiple_of(row, 128), 128), columns] = ebuf[part, rel, columns, :].T

    def enc_first(part, rel):
        for u in range(2):
            put_et(part, rel, u)

    def enc_second(u):
        pre[u].wait_recv()
        go(ecopy[1, 1, u])
        go(ecopy[1, 7, u])

    def enc_in(part, rel, u):
        ecopy[part, rel, u].wait_recv()
        top = 4 if part == u else 3
        if rel < top:
            go(ecopy[part, rel + 1, u])
        elif rel > top + 1:
            go(ecopy[part, rel - 1, u])
        put_et(part, rel, u)

    def z_part(part, t, pair, which):
        slot = {(0, 0): 0, (0, 1): 2, (1, 0): 1, (1, 1): 3}[part, which]
        rows = wq.at[which, pl.ds(pair * 256, 256), :]
        acc = None
        for h in range(4):
            term = dot(val[slot, h, t * 256 : (t + 1) * 256, :], rows[:, h * 256 : (h + 1) * 256], 1, 1)
            acc = term if acc is None else acc + term
        for i in range(2):
            half = acc[:, i * 128 : (i + 1) * 128]
            if which == 0:
                zsum[part, 2 * pair + i, t * 256 : (t + 1) * 256, :] = half
            else:
                zsum[part, 2 * pair + i, t * 256 : (t + 1) * 256, :] += half

    own_w_waits = list(own_w)

    def z_first(part, t):
        while own_w_waits:
            own_w_waits.pop().wait()
        for h in range(4):
            if part == 1:
                value_in(1, h, t)
        for pair in range(4):
            z_part(part, t, pair, 0)

    w_x, w_c = {}, {}
    for j in range(2):
        for k in range(3):
            ref = weight_piece(piece, j)
            w_x[k, j] = remote(ref, ref, wssem.at[1 + k, j], wrsem.at[1 + k, j], xdev[k])
        for k in range(4):
            ref = weight_piece(2 * ((x + 4 - k) % 4) + c, j)
            w_c[k, j] = remote(ref, ref, wssem.at[4 + k, j], wrsem.at[4 + k, j], peer)

    def weight_on(j):
        w_in[j].wait_recv()
        for k in (1, 0, 2):
            go(w_x[k, j])
        go(w_c[0, j])

    def weight_across(k, j):
        w_x[k, j].wait_recv()
        go(w_c[k + 1, j])

    zcopy = {}
    for part in range(2):
        for direction in range(2):
            for tau in range(4):
                for step in range(4 if direction == tau % 2 else 3):
                    zcopy[part, direction, tau, step] = remote(
                        zs.at[part, direction, tau, step], zr.at[part, direction, tau, step],
                        zssem.at[part, direction, tau, step], zrsem.at[part, direction, tau, step], zdev[direction],
                    )

    def z_step(part, direction, tau, step):
        length = 4 if direction == tau % 2 else 3
        if step >= length:
            return
        ahead = length - step
        slot = POS[(8 - ahead) % 8 if direction else ahead]
        value = zsum[part, slot, tau * 128 : (tau + 1) * 128, :]
        if step > 0:
            zcopy[part, direction, tau, step - 1].wait_recv()
            value = value + zr[part, direction, tau, step - 1].astype(F32)
        zs[part, direction, tau, step] = value.astype(BF16)
        go(zcopy[part, direction, tau, step])

    def z_start(part, t):
        for h in range(4):
            value_in(3 if part == 1 else 2, h, t)
        for pair in range(4):
            z_part(part, t, pair, 1)
            if pair == 0:
                z_step(part, 0, 2 * t, 0)
                z_step(part, 1, 2 * t + 1, 0)
                z_step(part, 0, 2 * t + 1, 0)
            if pair == 1:
                z_step(part, 1, 2 * t, 0)

    def z_on(part, t, step):
        z_step(part, 0, 2 * t, step)
        z_step(part, 1, 2 * t + 1, step)
        z_step(part, 0, 2 * t + 1, step)
        z_step(part, 1, 2 * t, step)

    def z_end(part, t):
        for tau in (2 * t, 2 * t + 1):
            rows = slice(tau * 128, (tau + 1) * 128)
            value = zsum[part, POS[0], rows, :]
            for direction in (1 - tau % 2, tau % 2):
                step = (4 if direction == tau % 2 else 3) - 1
                zcopy[part, direction, tau, step].wait_recv()
                value = value + zr[part, direction, tau, step].astype(F32)
            zout[part, rows, :] = value.astype(BF16)

    out_copy = remote(zout.at[1], enc_out.at[s], ossem.at[0], orsem.at[0], n1)
    own_copy = pltpu.make_async_copy(zout.at[0], enc_out.at[s], ossem.at[1])

    gcopy = [remote(gs.at[i], gr.at[i], gssem.at[i], grsem.at[i], peer) for i in range(8)]

    def g_head(f, h):
        i = f * 4 + h
        va, vb = (0, 1) if f == 0 else (2, 3)
        for t in range(2):
            if f == 1:
                value_in(va, h, t)
            value_in(vb, h, t)
        gs[i] = (dot(et[0, 512:, :], val[va, h], 1, 0) + dot(et[1, 512:, :], val[vb, h], 1, 0)).astype(BF16)
        go(gcopy[i])
        gkeep[i] = dot(et[0, :512, :], val[va, h], 1, 0) + dot(et[1, :512, :], val[vb, h], 1, 0)

    xcopy = {}
    for i in range(8):
        for k in range(3):
            xcopy[i, k] = remote(xs.at[i, k], xr.at[i, k], xssem.at[i, k], xrsem.at[i, k], xdev[k])

    def x_send(f, h):
        i = f * 4 + h
        gcopy[i].wait_recv()
        for k in (1, 0, 2):
            rows = slice((k + 1) * 128, (k + 2) * 128)
            xs[i, k] = (gkeep[i, rows, :] + gr[i, rows, :].astype(F32)).astype(BF16)
            go(xcopy[i, k])

    fcopy, flocal = {}, {}
    for i in range(8):
        where = dev(x, c, m, z, m if i < 4 else 1 - m)
        fcopy[i] = remote(fs.at[i], val_out.at[s, i % 4], fssem.at[i], frsem.at[s, i % 4], where)
        flocal[i] = pltpu.make_async_copy(fs.at[i], val_out.at[s, i % 4], frsem.at[s, i % 4])

    def f_send(f, h):
        i = f * 4 + h
        value = gkeep[i, :128, :] + gr[i, :128, :].astype(F32)
        for k in range(3):
            xcopy[i, k].wait_recv()
            value = value + xr[i, k].astype(F32)
        fs[i] = value.astype(BF16)
        if f == 0:
            @pl.when(selfy)
            def _():
                flocal[i].start()

            @pl.when(jnp.logical_not(selfy))
            def _():
                fcopy[i].start()
        else:
            go(fcopy[i])

    def f_in(h):
        for half in range(2):
            remote(fs.at[h], val_out.at[half, h], fssem.at[h], frsem.at[half, h], n1).wait_recv()

    def value_on(to, i):
        if to == 3 and i < WINDOW:
            sent(w_in[i - 1])
        value_next(to, i)

    def weights_in():
        for copy in w_c.values():
            copy.wait_recv()

    steps = {
        "et": enc_first, "second": enc_second, "e": enc_in, "v": value_on, "won": weight_on, "wac": weight_across,
        "wdone": weights_in, "zf": z_first, "zs": z_start, "z": z_step, "ze": z_end, "out": lambda: go(out_copy),
        "g": g_head, "x": x_send, "f": f_send, "fin": f_in,
    }
    for what, *which in ORDER:
        steps[what](*which)
    own_copy.start()
    out_copy.wait_recv()
    for copy in sends:
        copy.wait_send()
    for i in range(4):
        @pl.when(jnp.logical_not(selfy))
        def _():
            fcopy[i].wait_send()
    own_copy.wait()


def finish(enc_in, val_in, eg_out, vg_out):
    for half in range(2):
        eg_out[:, half * 128 : (half + 1) * 128] = enc_in[half]
        for h in range(4):
            vg_out[0, half * 128 : (half + 1) * 128, h * 256 : (h + 1) * 256] = val_in[half, h].astype(F32)


def local(enc_states, value_weight, attn_weights, ctx_grad, prompt_lengths):
    anywhere = pl.BlockSpec(memory_space=pl.ANY)
    vmem = pl.BlockSpec(memory_space=pltpu.VMEM)
    dma = pltpu.SemaphoreType.DMA
    enc_halves, value_parts = pl.pallas_call(
        kernel,
        out_shape=(jax.ShapeDtypeStruct((2, 512, 128), BF16), jax.ShapeDtypeStruct((2, 4, 128, 256), BF16)),
        in_specs=[pl.BlockSpec(memory_space=pltpu.SMEM)] + [anywhere] * 4,
        out_specs=(anywhere, anywhere),
        scratch_shapes=[
            pltpu.VMEM((4, 256, 512), BF16),
            pltpu.VMEM((256, 1024), BF16),
            pltpu.VMEM((2, 8, 512, 128), BF16),
            pltpu.VMEM((2, 1024, 512), BF16),
            pltpu.VMEM((4, 4, 512, 256), BF16),
            pltpu.VMEM((2, 1024, 1024), BF16),
            pltpu.VMEM((2, 8, 512, 128), F32),
            pltpu.VMEM((2, 2, 4, 4, 128, 128), BF16),
            pltpu.VMEM((2, 2, 4, 4, 128, 128), BF16),
            pltpu.VMEM((8, 512, 256), F32),
            pltpu.VMEM((8, 512, 256), BF16),
            pltpu.VMEM((8, 512, 256), BF16),
            pltpu.VMEM((8, 3, 128, 256), BF16),
            pltpu.VMEM((8, 3, 128, 256), BF16),
            pltpu.VMEM((8, 128, 256), BF16),
            pltpu.VMEM((2, 512, 128), BF16),
            dma((6,)), dma((8,)),
            dma((2, 8, 2)), dma((2, 8, 2)),
            dma((4, 4, 2)), dma((4, 4, 2)),
            dma((8, 2)), dma((8, 2)),
            dma((2, 2, 4, 4)), dma((2, 2, 4, 4)),
            dma((8,)), dma((8,)),
            dma((8, 3)), dma((8, 3)),
            dma((8,)), dma((2, 4)),
            dma((2,)), dma((1,)),
        ],
        compiler_params=pltpu.CompilerParams(
            collective_id=0, has_side_effects=True, vmem_limit_bytes=60 * 2**20
        ),
        cost_estimate=pl.CostEstimate(flops=9 * 10**9, bytes_accessed=12 * 2**20, transcendentals=0),
    )(prompt_lengths, enc_states, value_weight, attn_weights, ctx_grad)
    return pl.pallas_call(
        finish,
        out_shape=(jax.ShapeDtypeStruct((512, 256), BF16), jax.ShapeDtypeStruct((1, 256, 1024), F32)),
        in_specs=[vmem, vmem],
        out_specs=(vmem, vmem),
    )(enc_halves, value_parts)


def solution(mesh):
    in_specs = (
        P("dp", ("section", "mp")),
        P("section", None, "mp"),
        P("section", "mp", "dp", None),
        P("section", "dp", "mp"),
        P("dp"),
    )
    out_specs = (P("dp", ("section", "mp")), P("section", "dp", "mp"))
    return jax.shard_map(local, mesh=mesh, in_specs=in_specs, out_specs=out_specs, check_vma=False)
```

time: 541 us -> 77 us (0.14)
  waiting for transfers between devices: 494 us -> 0 us
  Pallas kernels: 0 us -> 75.6 us
  matrix products: 24.5 us -> 0 us
  between operations: 14.4 us -> 1.29 us
    reduce_scatter x2 -> x0, waiting for transfers between devices: 400 us -> none  [the longest x1 214 us: local(): lax.psum_scatter(partial_enc, ('section', 'mp'), scatter_dimension=1, til...]
    all_gather x1 -> x0, waiting for transfers between devices: 92.5 us -> none  [local(): encoded = lax.all_gather(enc_states, ('section', 'mp'), axis=1, tiled=True)]
    pallas_call x0 -> x2, Pallas kernels: none -> 75.6 us  [the longest x1 73.3 us: local(): pl.pallas_call(kernel, out_shape=(jax.ShapeDtypeStruct((2, 512, 128), BF1...]
    dot_general x3 -> x0, matrix products: 24.5 us -> none  [the longest x1 12.7 us: local(): lax.dot_general(encoded, value_grads, (((0,), (0,)), ((), ())), preferred...]
  transfers between devices with their start and end apart: 3 -> 0, of which waited for: 3 -> 0; matrix products, arithmetic and copies ran while one was open for 5% -> 0% of each run, Pallas kernels for 0% -> 0%
where the time goes in v2:
time: 77 us; the launch traced here: 76.9 us
  Pallas kernels  75.6 us (98%)
  between operations  1.29 us (2%)
    pallas_call x1, Pallas kernels, local(): pl.pallas_call(kernel, out_shape=(jax.ShapeDtypeStruct((2, 512, 128), BF1...  73.3 us
    pallas_call x1, Pallas kernels, local(): pl.pallas_call(finish, out_shape=(jax.ShapeDtypeStruct((512, 256), BF16),...  2.26 us

profile of v2, /device:TPU:1, one launch (start us, length us, event | category | flops | bytes accessed | tf_op | source)
XLA Modules:
  0.0 76.9 jit_solution(8734727786434669948)
XLA Ops:
  1.3 73.3 %shard_map.68 = (bf16[2,512,128]{2,1,0:T(8,128)(2,1)}, bf16[2,4,128,256]{3,2,1,0:T(8,128)(2,1)}) custom-call(s32[1]{0:T(128)S(6)} %copy.7.lens, bf16[512,256]{1,0:T(8,128)(2,1)} %enc.1, bf16[1,4096,1024]{2,1,0:T(8,128)(2,1)} %weight.1, bf16[1,4,256,512]{3,2,1,0:T(8,128)(2,1)} %attn.1, bf16[1,256,1024]{2,1,0:T(8,128)(2,1)} %ctx.1), custom_call_target="tpu_custom_call" | custom-call | flops 8999999488 | bytes 12582912 | tf_op jit(solution)/shard_map/pallas_call | solution.py:406
  74.6 2.3 %shard_map.69 = (bf16[512,256]{1,0:T(8,128)(2,1)}, f32[1,256,1024]{2,1,0:T(8,128)}) custom-call(bf16[2,512,128]{2,1,0:T(8,128)(2,1)} %get-tuple-element.4.enc_in, bf16[2,4,128,256]{3,2,1,0:T(8,128)(2,1)} %get-tuple-element.5.val_in), custom_call_target="tpu_custom_call" | custom-call | tf_op jit(solution)/shard_map/pallas_call | solution.py:443

commit v3 on v2

--- a/solution.py
+++ b/solution.py
@@ -11,29 +11,28 @@
 POS = {rel: slot for slot, rel in enumerate(REL)}
 BF16 = jnp.bfloat16
 F32 = jnp.float32
-WINDOW = 3
+WINDOW = 8
 ORDER = (
-    ("v", 3, 1), ("second", 0), ("et", 0, 0), ("zf", 0, 0), ("e", 0, 1, 0), ("e", 0, 7, 0), ("zf", 0, 1), ("won", 0),
-    ("v", 3, 2), ("v", 1, 3), ("second", 1), ("et", 1, 0), ("e", 0, 1, 1), ("e", 0, 7, 1), ("e", 1, 7, 0),
-    ("e", 1, 1, 0), ("won", 1), ("v", 3, 3), ("v", 1, 4), ("e", 0, 6, 0), ("e", 0, 2, 0), ("e", 1, 1, 1),
-    ("e", 1, 7, 1), ("v", 1, 5), ("v", 3, 4), ("wac", 1, 0), ("e", 0, 2, 1), ("e", 0, 6, 1), ("e", 1, 2, 0),
-    ("e", 1, 6, 0), ("v", 1, 6), ("v", 3, 5), ("wac", 2, 0), ("wac", 0, 0), ("e", 0, 5, 0), ("e", 0, 3, 0),
-    ("e", 1, 2, 1), ("zf", 1, 0), ("wac", 1, 1), ("v", 1, 7), ("v", 3, 6), ("e", 1, 6, 1), ("e", 0, 3, 1),
-    ("e", 0, 5, 1), ("e", 1, 5, 0), ("e", 1, 3, 0), ("v", 1, 8), ("v", 3, 7), ("wac", 2, 1), ("wac", 0, 1),
-    ("e", 0, 4, 0), ("wdone",), ("zs", 1, 0), ("e", 1, 3, 1), ("e", 1, 5, 1), ("v", 1, 9), ("v", 3, 8),
-    ("e", 0, 4, 1), ("e", 1, 4, 0), ("v", 1, 10), ("v", 3, 9), ("z", 1, 1, 0, 1), ("z", 1, 0, 0, 1),
-    ("z", 1, 0, 1, 1), ("z", 1, 1, 1, 1), ("e", 1, 4, 1), ("g", 0, 0), ("g", 0, 1), ("z", 1, 0, 0, 2),
-    ("z", 1, 0, 1, 2), ("v", 3, 10), ("x", 0, 0), ("zf", 1, 1), ("v", 3, 11), ("x", 0, 1), ("v", 1, 11),
-    ("z", 1, 1, 0, 2), ("z", 1, 1, 1, 2), ("g", 0, 3), ("zs", 1, 1), ("z", 1, 0, 0, 3), ("g", 0, 2), ("x", 0, 3),
-    ("g", 1, 0), ("x", 0, 2), ("g", 1, 1), ("z", 1, 1, 3, 1), ("z", 1, 1, 2, 1), ("x", 1, 0), ("z", 1, 0, 2, 1),
-    ("f", 0, 1), ("z", 1, 0, 3, 1), ("zs", 0, 0), ("z", 1, 1, 1, 3), ("f", 0, 0), ("g", 1, 2), ("z", 1, 1, 3, 2),
-    ("zs", 0, 1), ("z", 1, 1, 2, 2), ("z", 1, 0, 3, 2), ("x", 1, 2), ("z", 1, 0, 2, 2), ("z", 0, 1, 0, 1),
-    ("f", 0, 3), ("z", 0, 0, 0, 1), ("x", 1, 1), ("z", 0, 0, 1, 1), ("f", 0, 2), ("z", 0, 1, 1, 1), ("ze", 1, 0),
-    ("g", 1, 3), ("z", 1, 1, 3, 3), ("z", 0, 1, 2, 1), ("z", 0, 0, 2, 1), ("z", 0, 0, 3, 1), ("z", 0, 1, 3, 1),
-    ("f", 1, 0), ("x", 1, 3), ("z", 1, 0, 2, 3), ("z", 0, 1, 0, 2), ("z", 0, 0, 0, 2), ("z", 0, 1, 1, 2),
-    ("z", 0, 0, 1, 2), ("f", 1, 2), ("z", 0, 0, 2, 2), ("z", 0, 1, 2, 2), ("fin", 0), ("z", 0, 0, 3, 2),
-    ("z", 0, 1, 3, 2), ("ze", 1, 1), ("out",), ("z", 0, 0, 0, 3), ("f", 1, 1), ("z", 0, 1, 1, 3), ("fin", 2),
-    ("z", 0, 0, 2, 3), ("z", 0, 1, 3, 3), ("f", 1, 3), ("ze", 0, 0), ("fin", 1), ("ze", 0, 1), ("fin", 3),
+    ("second", 0), ("v", 3, 4), ("zf", 0, 1), ("v", 3, 1), ("v", 3, 2), ("v", 3, 3), ("zf", 0, 0), ("e", 0, 1, 0),
+    ("second", 1), ("e", 0, 7, 0), ("won", 0), ("v", 3, 5), ("v", 3, 6), ("et", 1, 0), ("v", 3, 7), ("et", 0, 0),
+    ("e", 0, 1, 1), ("e", 0, 7, 1), ("e", 1, 7, 0), ("e", 1, 1, 0), ("won", 1), ("e", 0, 2, 0), ("e", 1, 7, 1),
+    ("e", 1, 1, 1), ("e", 0, 6, 0), ("v", 1, 8), ("wac", 1, 0), ("e", 0, 2, 1), ("e", 0, 6, 1), ("e", 1, 2, 0),
+    ("e", 1, 6, 0), ("wac", 0, 0), ("wac", 2, 0), ("e", 0, 3, 0), ("e", 1, 6, 1), ("e", 1, 2, 1), ("e", 0, 5, 0),
+    ("wac", 1, 1), ("v", 1, 9), ("zf", 1, 0), ("e", 0, 3, 1), ("e", 0, 5, 1), ("e", 1, 3, 0), ("e", 1, 5, 0),
+    ("v", 3, 8), ("wac", 2, 1), ("v", 1, 10), ("wac", 0, 1), ("e", 0, 4, 0), ("e", 1, 5, 1), ("wdone",),
+    ("e", 1, 3, 1), ("v", 3, 9), ("v", 1, 11), ("e", 0, 4, 1), ("zs", 1, 0), ("e", 1, 4, 0), ("v", 3, 10),
+    ("e", 1, 4, 1), ("g", 0, 2), ("z", 1, 1, 0, 1), ("z", 1, 1, 1, 1), ("z", 1, 0, 0, 1), ("g", 0, 0), ("zf", 1, 1),
+    ("x", 0, 2), ("z", 1, 0, 1, 1), ("v", 3, 11), ("g", 0, 3), ("x", 0, 0), ("g", 0, 1), ("z", 1, 1, 0, 2),
+    ("zs", 1, 1), ("x", 0, 3), ("z", 1, 1, 1, 2), ("z", 1, 0, 0, 2), ("x", 0, 1), ("z", 1, 0, 1, 2), ("g", 1, 0),
+    ("z", 1, 0, 2, 1), ("z", 1, 1, 2, 1), ("x", 1, 0), ("z", 1, 1, 3, 1), ("z", 1, 0, 3, 1), ("g", 1, 1),
+    ("z", 1, 0, 0, 3), ("z", 1, 1, 1, 3), ("x", 1, 1), ("z", 1, 0, 2, 2), ("z", 1, 1, 2, 2), ("zs", 0, 0),
+    ("z", 1, 1, 3, 2), ("z", 1, 0, 3, 2), ("g", 1, 2), ("ze", 1, 0), ("f", 0, 0), ("zs", 0, 1), ("f", 0, 2),
+    ("x", 1, 2), ("z", 0, 1, 0, 1), ("z", 0, 0, 0, 1), ("z", 1, 0, 2, 3), ("g", 1, 3), ("z", 0, 1, 1, 1),
+    ("z", 0, 0, 1, 1), ("f", 0, 3), ("z", 1, 1, 3, 3), ("f", 0, 1), ("x", 1, 3), ("f", 1, 0), ("z", 0, 1, 2, 1),
+    ("z", 0, 0, 2, 1), ("z", 0, 0, 3, 1), ("z", 0, 1, 3, 1), ("z", 0, 1, 0, 2), ("z", 0, 0, 0, 2), ("z", 0, 1, 1, 2),
+    ("f", 1, 1), ("z", 0, 0, 1, 2), ("ze", 1, 1), ("out",), ("fin", 0), ("z", 0, 1, 2, 2), ("z", 0, 0, 2, 2),
+    ("z", 0, 1, 3, 2), ("z", 0, 0, 3, 2), ("z", 0, 0, 0, 3), ("f", 1, 2), ("z", 0, 1, 1, 3), ("fin", 1),
+    ("z", 0, 0, 2, 3), ("z", 0, 1, 3, 3), ("f", 1, 3), ("ze", 0, 0), ("fin", 2), ("ze", 0, 1), ("fin", 3),
 )
 
 
@@ -188,6 +187,8 @@
             value_next(1, h)
         if h == 0:
             value_next(3, 0)
+    for i in range(4, WINDOW):
+        value_next(1, i)
 
     def put_et(part, rel, u):
         layer = (z + 8 - rel) % 8
@@ -365,9 +366,14 @@
         for half in range(2):
             remote(fs.at[h], val_out.at[half, h], fssem.at[h], frsem.at[half, h], n1).wait_recv()
 
+    w_left = [0, 1]
+
     def value_on(to, i):
         if to == 3 and i < WINDOW:
-            sent(w_in[i - 1])
+            j = 0 if i <= WINDOW // 2 else 1
+            if j in w_left:
+                w_left.remove(j)
+                sent(w_in[j])
         value_next(to, i)
 
     def weights_in():

time: 77 us -> 76.1 us (0.988)
  Pallas kernels: 75.6 us -> 74.7 us
    pallas_call x1, Pallas kernels: 73.3 us -> 72.4 us  [local(): pl.pallas_call(kernel, out_shape=(jax.ShapeDtypeStruct((2, 512, 128), BF1...]
where the time goes in v3:
time: 76.1 us; the launch traced here: 76 us
  Pallas kernels  74.7 us (98%)
  between operations  1.29 us (2%)
    pallas_call x1, Pallas kernels, local(): pl.pallas_call(kernel, out_shape=(jax.ShapeDtypeStruct((2, 512, 128), BF1...  72.4 us
    pallas_call x1, Pallas kernels, local(): pl.pallas_call(finish, out_shape=(jax.ShapeDtypeStruct((512, 256), BF16),...  2.26 us

profile of v3, /device:TPU:1, one launch (start us, length us, event | category | flops | bytes accessed | tf_op | source)
XLA Modules:
  0.0 76.0 jit_solution(10188413604474541062)
XLA Ops:
  1.3 72.4 %shard_map.68 = (bf16[2,512,128]{2,1,0:T(8,128)(2,1)}, bf16[2,4,128,256]{3,2,1,0:T(8,128)(2,1)}) custom-call(s32[1]{0:T(128)S(6)} %copy.7.lens, bf16[512,256]{1,0:T(8,128)(2,1)} %enc.1, bf16[1,4096,1024]{2,1,0:T(8,128)(2,1)} %weight.1, bf16[1,4,256,512]{3,2,1,0:T(8,128)(2,1)} %attn.1, bf16[1,256,1024]{2,1,0:T(8,128)(2,1)} %ctx.1), custom_call_target="tpu_custom_call" | custom-call | flops 8999999488 | bytes 12582912 | tf_op jit(solution)/shard_map/pallas_call | solution.py:412
  73.7 2.3 %shard_map.69 = (bf16[512,256]{1,0:T(8,128)(2,1)}, f32[1,256,1024]{2,1,0:T(8,128)}) custom-call(bf16[2,512,128]{2,1,0:T(8,128)(2,1)} %get-tuple-element.4.enc_in, bf16[2,4,128,256]{3,2,1,0:T(8,128)(2,1)} %get-tuple-element.5.val_in), custom_call_target="tpu_custom_call" | custom-call | tf_op jit(solution)/shard_map/pallas_call | solution.py:449

commit v4 on v3

--- a/solution.py
+++ b/solution.py
@@ -11,28 +11,29 @@
 POS = {rel: slot for slot, rel in enumerate(REL)}
 BF16 = jnp.bfloat16
 F32 = jnp.float32
-WINDOW = 8
+WINDOW = 5
 ORDER = (
-    ("second", 0), ("v", 3, 4), ("zf", 0, 1), ("v", 3, 1), ("v", 3, 2), ("v", 3, 3), ("zf", 0, 0), ("e", 0, 1, 0),
-    ("second", 1), ("e", 0, 7, 0), ("won", 0), ("v", 3, 5), ("v", 3, 6), ("et", 1, 0), ("v", 3, 7), ("et", 0, 0),
-    ("e", 0, 1, 1), ("e", 0, 7, 1), ("e", 1, 7, 0), ("e", 1, 1, 0), ("won", 1), ("e", 0, 2, 0), ("e", 1, 7, 1),
-    ("e", 1, 1, 1), ("e", 0, 6, 0), ("v", 1, 8), ("wac", 1, 0), ("e", 0, 2, 1), ("e", 0, 6, 1), ("e", 1, 2, 0),
-    ("e", 1, 6, 0), ("wac", 0, 0), ("wac", 2, 0), ("e", 0, 3, 0), ("e", 1, 6, 1), ("e", 1, 2, 1), ("e", 0, 5, 0),
-    ("wac", 1, 1), ("v", 1, 9), ("zf", 1, 0), ("e", 0, 3, 1), ("e", 0, 5, 1), ("e", 1, 3, 0), ("e", 1, 5, 0),
-    ("v", 3, 8), ("wac", 2, 1), ("v", 1, 10), ("wac", 0, 1), ("e", 0, 4, 0), ("e", 1, 5, 1), ("wdone",),
-    ("e", 1, 3, 1), ("v", 3, 9), ("v", 1, 11), ("e", 0, 4, 1), ("zs", 1, 0), ("e", 1, 4, 0), ("v", 3, 10),
-    ("e", 1, 4, 1), ("g", 0, 2), ("z", 1, 1, 0, 1), ("z", 1, 1, 1, 1), ("z", 1, 0, 0, 1), ("g", 0, 0), ("zf", 1, 1),
-    ("x", 0, 2), ("z", 1, 0, 1, 1), ("v", 3, 11), ("g", 0, 3), ("x", 0, 0), ("g", 0, 1), ("z", 1, 1, 0, 2),
-    ("zs", 1, 1), ("x", 0, 3), ("z", 1, 1, 1, 2), ("z", 1, 0, 0, 2), ("x", 0, 1), ("z", 1, 0, 1, 2), ("g", 1, 0),
-    ("z", 1, 0, 2, 1), ("z", 1, 1, 2, 1), ("x", 1, 0), ("z", 1, 1, 3, 1), ("z", 1, 0, 3, 1), ("g", 1, 1),
-    ("z", 1, 0, 0, 3), ("z", 1, 1, 1, 3), ("x", 1, 1), ("z", 1, 0, 2, 2), ("z", 1, 1, 2, 2), ("zs", 0, 0),
-    ("z", 1, 1, 3, 2), ("z", 1, 0, 3, 2), ("g", 1, 2), ("ze", 1, 0), ("f", 0, 0), ("zs", 0, 1), ("f", 0, 2),
-    ("x", 1, 2), ("z", 0, 1, 0, 1), ("z", 0, 0, 0, 1), ("z", 1, 0, 2, 3), ("g", 1, 3), ("z", 0, 1, 1, 1),
-    ("z", 0, 0, 1, 1), ("f", 0, 3), ("z", 1, 1, 3, 3), ("f", 0, 1), ("x", 1, 3), ("f", 1, 0), ("z", 0, 1, 2, 1),
-    ("z", 0, 0, 2, 1), ("z", 0, 0, 3, 1), ("z", 0, 1, 3, 1), ("z", 0, 1, 0, 2), ("z", 0, 0, 0, 2), ("z", 0, 1, 1, 2),
-    ("f", 1, 1), ("z", 0, 0, 1, 2), ("ze", 1, 1), ("out",), ("fin", 0), ("z", 0, 1, 2, 2), ("z", 0, 0, 2, 2),
-    ("z", 0, 1, 3, 2), ("z", 0, 0, 3, 2), ("z", 0, 0, 0, 3), ("f", 1, 2), ("z", 0, 1, 1, 3), ("fin", 1),
-    ("z", 0, 0, 2, 3), ("z", 0, 1, 3, 3), ("f", 1, 3), ("ze", 0, 0), ("fin", 2), ("ze", 0, 1), ("fin", 3),
+    ("v", 3, 1), ("second", 0), ("v", 3, 2), ("zf", 0, 1), ("et", 0, 0), ("zf", 0, 0), ("e", 0, 1, 0), ("second", 1),
+    ("won", 0), ("v", 1, 5), ("v", 3, 3), ("v", 3, 4), ("e", 0, 7, 0), ("et", 1, 0), ("e", 0, 1, 1), ("e", 0, 7, 1),
+    ("e", 1, 1, 0), ("e", 1, 7, 0), ("won", 1), ("v", 3, 5), ("v", 1, 6), ("e", 0, 2, 0), ("e", 1, 7, 1),
+    ("e", 1, 1, 1), ("e", 0, 6, 0), ("v", 3, 6), ("v", 1, 7), ("wac", 1, 0), ("e", 0, 2, 1), ("e", 0, 6, 1),
+    ("e", 1, 2, 0), ("e", 1, 6, 0), ("wac", 2, 0), ("wac", 0, 0), ("v", 1, 8), ("v", 3, 7), ("e", 0, 3, 0),
+    ("e", 1, 6, 1), ("e", 1, 2, 1), ("e", 0, 5, 0), ("v", 3, 8), ("wac", 1, 1), ("e", 0, 3, 1), ("e", 0, 5, 1),
+    ("e", 1, 3, 0), ("e", 1, 5, 0), ("wac", 2, 1), ("wac", 0, 1), ("v", 1, 10), ("zf", 1, 0), ("e", 0, 4, 0),
+    ("e", 1, 5, 1), ("wdone",), ("e", 1, 3, 1), ("v", 3, 10), ("zs", 1, 0), ("e", 0, 4, 1), ("e", 1, 4, 0),
+    ("v", 1, 9), ("e", 1, 4, 1), ("g", 0, 1), ("z", 1, 1, 0, 1), ("g", 0, 0), ("v", 3, 9), ("z", 1, 0, 1, 1),
+    ("z", 1, 1, 1, 1), ("g", 0, 2), ("z", 1, 0, 0, 1), ("x", 0, 1), ("v", 1, 11), ("x", 0, 0), ("x", 0, 2),
+    ("z", 1, 1, 0, 2), ("v", 3, 11), ("zf", 1, 1), ("g", 0, 3), ("z", 1, 1, 1, 2), ("z", 1, 0, 1, 2),
+    ("z", 1, 0, 0, 2), ("x", 0, 3), ("zs", 1, 1), ("z", 1, 1, 1, 3), ("z", 1, 0, 0, 3), ("z", 1, 0, 2, 1),
+    ("z", 1, 1, 2, 1), ("z", 1, 0, 3, 1), ("z", 1, 1, 3, 1), ("g", 1, 0), ("zs", 0, 0), ("ze", 1, 0), ("x", 1, 0),
+    ("z", 1, 1, 2, 2), ("z", 1, 0, 2, 2), ("z", 1, 0, 3, 2), ("z", 1, 1, 3, 2), ("g", 1, 1), ("g", 1, 2),
+    ("z", 0, 1, 0, 1), ("z", 0, 0, 0, 1), ("x", 1, 1), ("z", 0, 1, 1, 1), ("z", 0, 0, 1, 1), ("zs", 0, 1),
+    ("z", 1, 0, 2, 3), ("x", 1, 2), ("f", 0, 0), ("z", 1, 1, 3, 3), ("g", 1, 3), ("f", 0, 1), ("f", 1, 0),
+    ("f", 0, 3), ("z", 0, 1, 0, 2), ("z", 0, 0, 0, 2), ("f", 0, 2), ("z", 0, 1, 1, 2), ("z", 0, 0, 1, 2), ("x", 1, 3),
+    ("z", 0, 1, 2, 1), ("z", 0, 0, 2, 1), ("z", 0, 1, 3, 1), ("z", 0, 0, 3, 1), ("f", 1, 1), ("ze", 1, 1), ("out",),
+    ("z", 0, 0, 0, 3), ("fin", 0), ("z", 0, 1, 1, 3), ("z", 0, 1, 2, 2), ("z", 0, 0, 2, 2), ("f", 1, 2),
+    ("z", 0, 1, 3, 2), ("z", 0, 0, 3, 2), ("fin", 1), ("ze", 0, 0), ("f", 1, 3), ("z", 0, 0, 2, 3), ("z", 0, 1, 3, 3),
+    ("fin", 2), ("fin", 3), ("ze", 0, 1),
 )
 
 
@@ -158,10 +159,10 @@
         for t in range(2):
             vcopy[1, h, t] = value_copy(0, 1, h, t, n1)
             vcopy[3, h, t] = value_copy(0, 3, h, t, n2)
-            vcopy[2, h, t] = value_copy(3, 2, h, t, n1) if t == 0 else value_copy(1, 2, h, t, n2)
+            vcopy[2, h, t] = value_copy(3, 2, h, t, n1) if h < 2 else value_copy(1, 2, h, t, n2)
     queues = {}
-    for to, through in ((1, 0), (3, 1)):
-        queues[to] = [(to, h, t) for t in range(2) for h in range(4)] + [(2, h, through) for h in range(4)]
+    for to, through in ((1, (0, 1)), (3, (2, 3))):
+        queues[to] = [(to, h, t) for t in range(2) for h in range(4)] + [(2, h, t) for h in through for t in range(2)]
     arrived = set()
 
     def value_in(*key):

time: 76.1 us -> 78.1 us (1.026)
  Pallas kernels: 74.7 us -> 76.7 us
    pallas_call x1, Pallas kernels: 72.4 us -> 74.4 us  [local(): pl.pallas_call(kernel, out_shape=(jax.ShapeDtypeStruct((2, 512, 128), BF1...]
where the time goes in v4:
time: 78.1 us; the launch traced here: 78 us
  Pallas kernels  76.7 us (98%)
  between operations  1.29 us (2%)
    pallas_call x1, Pallas kernels, local(): pl.pallas_call(kernel, out_shape=(jax.ShapeDtypeStruct((2, 512, 128), BF1...  74.4 us
    pallas_call x1, Pallas kernels, local(): pl.pallas_call(finish, out_shape=(jax.ShapeDtypeStruct((512, 256), BF16),...  2.26 us

profile of v4, /device:TPU:1, one launch (start us, length us, event | category | flops | bytes accessed | tf_op | source)
XLA Modules:
  0.0 78.0 jit_solution(14702078979406243650)
XLA Ops:
  1.3 74.4 %shard_map.68 = (bf16[2,512,128]{2,1,0:T(8,128)(2,1)}, bf16[2,4,128,256]{3,2,1,0:T(8,128)(2,1)}) custom-call(s32[1]{0:T(128)S(6)} %copy.7.lens, bf16[512,256]{1,0:T(8,128)(2,1)} %enc.1, bf16[1,4096,1024]{2,1,0:T(8,128)(2,1)} %weight.1, bf16[1,4,256,512]{3,2,1,0:T(8,128)(2,1)} %attn.1, bf16[1,256,1024]{2,1,0:T(8,128)(2,1)} %ctx.1), custom_call_target="tpu_custom_call" | custom-call | flops 8999999488 | bytes 12582912 | tf_op jit(solution)/shard_map/pallas_call | solution.py:413
  75.7 2.3 %shard_map.69 = (bf16[512,256]{1,0:T(8,128)(2,1)}, f32[1,256,1024]{2,1,0:T(8,128)}) custom-call(bf16[2,512,128]{2,1,0:T(8,128)(2,1)} %get-tuple-element.4.enc_in, bf16[2,4,128,256]{3,2,1,0:T(8,128)(2,1)} %get-tuple-element.5.val_in), custom_call_target="tpu_custom_call" | custom-call | tf_op jit(solution)/shard_map/pallas_call | solution.py:450
